TPU v7x, 32 devices: a whole 2x2x4 slice. The times are simulated.
32 devices in a mesh: row: 4 (over x, core), col: 8 (over z, y).
Axes of the slice: x: 2, y: 2, z: 4, core: 2. Of those that a mesh axis runs over, the one named last changes fastest.
Arguments:
- field_slab: float32 [672, 8, 4096], P('row', 'col'), may hold values from -16 to 16
- start_basis: float32 [672, 64], replicated, may hold values from -6 to 6
Outputs:
- core_tensor: float32 [64, 8, 4096], P(None, 'col', 'row')
- leading: float32 [672, 64], replicated
All inputs are finite; a program needn't handle non-finite values.
Results may differ from a plain program's by a relative error of at most 0.0003.
Values sent between devices are 32-bit elements; how exact they have to be, the bound alone decides.
A program may use at most 64 MiB of HBM per device.

v0:
```python
import functools

import jax
import jax.numpy as jnp
from jax import lax
from jax.experimental import pallas as pl
from jax.experimental.pallas import tpu as pltpu
from jax.sharding import PartitionSpec as P

ITERS = 8
HIGHEST = lax.Precision.HIGHEST


def dot(a, b):
    return jnp.dot(a, b, precision=HIGHEST, preferred_element_type=jnp.float32)


def dot_nt(a, b):
    return lax.dot_general(
        a, b, (((1,), (1,)), ((), ())), precision=HIGHEST, preferred_element_type=jnp.float32
    )


def inverse_factor(corr):
    rank = corr.shape[0]
    count = rank // 8
    identity = (
        lax.broadcasted_iota(jnp.int32, (rank, rank), 0)
        == lax.broadcasted_iota(jnp.int32, (rank, rank), 1)
    ).astype(jnp.float32)
    work = jnp.concatenate([corr, identity], axis=1)
    wide = 2 * rank
    rows = [work[8 * i : 8 * i + 8, :] for i in range(count)]
    sub = lax.broadcasted_iota(jnp.int32, (8, wide), 0)
    done = []
    for p in range(count):
        cols = [
            [jnp.broadcast_to(rows[i][:, 8 * p + j : 8 * p + j + 1], (8, wide)) for j in range(8)]
            for i in range(p, count)
        ]
        pivots = jnp.ones((8, wide), jnp.float32)
        for j in range(8):
            pivot = jnp.broadcast_to(cols[0][j][j : j + 1, :], (8, wide))
            pivots = jnp.where(sub == j, pivot, pivots)
            inverse = 1.0 / pivot
            row = jnp.broadcast_to(rows[p][j : j + 1, :], (8, wide))
            upper = {
                m: jnp.broadcast_to(cols[0][m][j : j + 1, :], (8, wide)) for m in range(j + 1, 8)
            }
            for i in range(p, count):
                if i == p and j == 7:
                    continue
                scale = cols[i - p][j] * inverse
                if i == p:
                    scale = jnp.where(sub > j, scale, 0.0)
                for m in range(j + 1, 8):
                    cols[i - p][m] = cols[i - p][m] - scale * upper[m]
                rows[i] = rows[i] - scale * row
        root = lax.rsqrt(pivots)
        root = root * (1.5 - (0.5 * pivots * root) * root)
        done.append((rows[p] * root)[:, rank:])
    return jnp.concatenate(done, axis=0)


def iterate_kernel(gram_ref, start_ref, out_ref, mapped):
    gram = gram_ref[...]
    mapped[...] = dot(start_ref[...].T, gram)

    @pl.loop(0, ITERS - 1)
    def _(step):
        current = mapped[...]
        inverse = inverse_factor(dot_nt(current, current))
        mapped[...] = dot(inverse, dot(current, gram_ref[...]))

    current = mapped[...]
    inverse = inverse_factor(dot_nt(current, current))
    out_ref[...] = dot(inverse, current)


def iterate(gram, start):
    size, rank = start.shape
    return pl.pallas_call(
        iterate_kernel,
        out_shape=jax.ShapeDtypeStruct((rank, size), jnp.float32),
        in_specs=[pl.BlockSpec(memory_space=pltpu.VMEM)] * 2,
        out_specs=pl.BlockSpec(memory_space=pltpu.VMEM),
        scratch_shapes=[pltpu.VMEM((rank, size), jnp.float32)],
        compiler_params=pltpu.CompilerParams(vmem_limit_bytes=32 * 1024 * 1024),
        name="iterate",
    )(gram, start)


def shards(field_slab, start_basis):
    gathered = lax.all_to_all(field_slab, "row", split_axis=2, concat_axis=0, tiled=True)
    flat = gathered.reshape(gathered.shape[0], -1)
    local_gram = dot_nt(flat, flat)
    gram_total = lax.psum(local_gram, ("row", "col"))
    leading_t = iterate(gram_total, start_basis)
    core = dot(leading_t, flat)
    return (core.reshape((-1,) + gathered.shape[1:]), leading_t.T)


def solution(mesh):
    placed = (P("row", "col", None), P())
    return jax.shard_map(
        shards, mesh=mesh, in_specs=placed, out_specs=(P(None, "col", "row"), P()), check_vma=False
    )
```

profile of v0, /device:TPU:0, one launch (start us, length us, event | category | flops | bytes accessed | tf_op | source)
XLA Modules:
  0.0 271.7 jit_solution(12125201829748308393)
XLA Ops:
  7.2 0.0 all-reduce.2.cloned.1.call-start
  7.2 13.9 %copy.16 = f32[168,1,4096]{0,1,2:T(1,128)} copy(f32[168,1,4096]{2,1,0:T(1,128)} %param.2) | data formatting | bytes 5505024 | tf_op args[0]
  21.1 54.5 %all_to_all.15 = f32[168,1,4096]{0,1,2:T(1,128)} all-to-all(f32[168,1,4096]{0,1,2:T(1,128)} %copy.16), channel_id=1, replica_groups=mesh['row'=4,'col'=8] {'row'}, dimensions={2} | all-to-all | bytes 5505024 | tf_op jit(solution)/shard_map/all_to_all | solution.py:94
  75.6 9.2 %copy.17 = f32[168,1,4096]{2,0,1:T(8,128)S(1)} copy(f32[168,1,4096]{0,1,2:T(1,128)} %all_to_all.15) | data formatting | bytes 5505024 | tf_op jit(solution)/shard_map/all_to_all | solution.py:94
  84.8 3.4 %all_to_all.12 = f32[168,1,4,1024]{3,2,0,1:T(4,128)} reshape(f32[168,1,4096]{2,0,1:T(8,128)S(1)} %copy.17) | data formatting | bytes 5505024 | tf_op jit(solution)/shard_map/all_to_all | solution.py:94
  88.2 3.4 %copy.18 = f32[4,168,1,1024]{3,1,0,2:T(8,128)S(1)} copy(f32[4,168,1,1024]{3,0,1,2:T(4,128)} %bitcast.13) | data formatting | bytes 5505024 | tf_op jit(solution)/shard_map/all_to_all | solution.py:94
  91.6 0.0 copy-start.1
  91.6 8.0 %fusion = f32[672,672]{1,0:T(8,128)} fusion(f32[672,1024]{1,0:T(8,128)S(1)} %bitcast.11), kind=kOutput, calls=%fused_computation.1 | convolution fusion | flops 5549064192 | bytes 4558848 | tf_op jit(solution)/shard_map/dot_general | solution.py:19
  99.6 0.0 all-reduce.2.cloned.1.call-update
  99.6 0.0 copy-done.1
  99.7 0.2 copy.19.start_ref
  99.8 134.6 %all-reduce.2.cloned.1.call-done.gram_ref = f32[672,672]{1,0:T(8,128)} async-done(((f32[672,672]{1,0:T(8,128)}), f32[672,672]{1,0:T(8,128)}) %all-reduce.2.cloned.1.call-update) | async-done | bytes 1806352 | tf_op jit(solution)/shard_map/psum | solution.py:97
  234.4 0.0 copy-start
  234.4 1.6 copy-done
  236.0 25.2 %iterate.1 = f32[64,672]{1,0:T(8,128)} custom-call(f32[672,672]{1,0:T(8,128)S(1)} %copy-done, f32[672,64]{1,0:T(8,128)S(1)} %copy.19.start_ref), custom_call_target="tpu_custom_call" | custom-call | tf_op jit(solution)/shard_map/iterate/pallas_call | solution.py:82
  261.2 2.7 convolution_bitcast_fusion
  263.9 1.0 copy.20
Async XLA Ops:
  7.2 227.3 %all-reduce.2.cloned.1.call-start = ((), (), s32[]{:S(2)}) async-start(), calls=%async_computation.1 | async-start | bytes 4128768 | tf_op jit(solution)/shard_map/psum | solution.py:97
  91.6 8.1 %copy-start.1 = (f32[672,64]{0,1:T(8,128)S(1)}, f32[672,64]{0,1:T(8,128)}, u32[]{:S(2)}) copy-start(f32[672,64]{0,1:T(8,128)} %param.3) | copy-start | bytes 516100
  234.4 1.6 copy-start
Sparse Core Ops, SparseCore 0:
  99.8 134.6 all-reduce.1
where the time goes:
time: 273 us; the launch traced here: 272 us
  waiting for transfers between devices  135 us (49%)
  blocking collectives  54.5 us (20%)
  local copies, waits for them, and re-layouts  32.6 us (12%)
  Pallas kernels  25.2 us (9%)
  between operations  14.1 us (5%)
  matrix products  10.7 us (4%)
    psum x1, waiting for transfers between devices, shards(): gram_total = lax.psum(local_gram, ('row', 'col'))  135 us
    all_to_all x1, blocking collectives, shards(): lax.all_to_all(field_slab, 'row', split_axis=2, concat_axis=0, tiled=True)  54.5 us
    pallas_call x1, Pallas kernels, iterate(): pl.pallas_call(iterate_kernel, out_shape=jax.ShapeDtypeStruct((rank, size...  25.2 us
    unnamed x7, local copies, waits for them, and re-layouts  16.6 us
    all_to_all x3, local copies, waits for them, and re-layouts, shards(): lax.all_to_all(field_slab, 'row', split_axis=2, concat_axis=0, tiled=True)  16 us
    dot_general x1, matrix products, dot_nt(): lax.dot_general(a, b, (((1,), (1,)), ((), ())), precision=HIGHEST, prefer...  8.01 us
  transfers between devices with their start and end apart: 1, of which 1 were waited for; matrix products, arithmetic and copies ran while one was open for 0% of the time, Pallas kernels for 0%

commit v1 on v0

--- a/solution.py
+++ b/solution.py
@@ -62,9 +62,216 @@
     return jnp.concatenate(done, axis=0)
 
 
-def iterate_kernel(gram_ref, start_ref, out_ref, mapped):
-    gram = gram_ref[...]
-    mapped[...] = dot(start_ref[...].T, gram)
+LANES = 128
+CHUNK = 256
+MESH = pl.DeviceIdType.MESH
+
+
+def strips(size):
+    found, start = [], 0
+    for first in range(0, size, LANES):
+        width = min(LANES, size - first)
+        found.append((first, width, first + width, start))
+        start += first + width
+    return found, start
+
+
+def gram_kernel(
+    x_size, y_size, z_size, slab_ref, gathered_ref, packed_ref,
+    local, total, halves, send, arrive, own, out_sem, rs_send, rs_arrive, ag_send, ag_arrive,
+):
+    rows, columns = slab_ref.shape
+    row_size = 2 * x_size
+    width = columns // row_size
+    size = rows * row_size
+    row, col = lax.axis_index("row"), lax.axis_index("col")
+    x, core = row // 2, row % 2
+    z, y = col // y_size, col % y_size
+    groups = [
+        (2, core, lambda i: {"row": x * 2 + i}),
+        (x_size, x, lambda i: {"row": i * 2 + core}),
+        (y_size, y, lambda i: {"col": z * y_size + i}),
+        (z_size, z, lambda i: {"col": i * y_size + y}),
+    ]
+
+    barrier = pltpu.get_barrier_semaphore()
+    met = 0
+    others = [(dx, dc) for dx in range(x_size) for dc in range(2) if dx or dc]
+    for dx, dc in others:
+        to = ((x + dx) % x_size) * 2 + (core + dc) % 2
+        pl.semaphore_signal(barrier, inc=1, device_id={"row": to}, device_id_type=MESH)
+        met += 1
+    for count, index, place in groups[2:]:
+        for k in range(1, count):
+            pl.semaphore_signal(
+                barrier, inc=1, device_id=place((index + k) % count), device_id_type=MESH
+            )
+            met += 1
+    pl.semaphore_wait(barrier, met)
+
+    chunks = width // CHUNK
+
+    def block_copy(n, chunk):
+        dx, dc = others[n]
+        to = ((x + dx) % x_size) * 2 + (core + dc) % 2
+        return pltpu.make_async_remote_copy(
+            src_ref=slab_ref.at[:, pl.ds(pl.multiple_of(to * width + chunk * CHUNK, CHUNK), CHUNK)],
+            dst_ref=local.at[
+                pl.ds(pl.multiple_of(row * rows, 8), rows),
+                pl.ds(pl.multiple_of(chunk * CHUNK, CHUNK), CHUNK),
+            ],
+            send_sem=send.at[n, chunk],
+            recv_sem=arrive.at[n, chunk],
+            device_id={"row": to},
+            device_id_type=MESH,
+        )
+
+    for chunk in range(chunks):
+        for n in reversed(range(len(others))):
+            block_copy(n, chunk).start()
+    mine = pltpu.make_async_copy(
+        slab_ref.at[:, pl.ds(pl.multiple_of(row * width, width), width)],
+        local.at[pl.ds(pl.multiple_of(row * rows, 8), rows), :],
+        own,
+    )
+    mine.start()
+    total[...] = jnp.zeros_like(total)
+    mine.wait()
+    spans, used = strips(size)
+
+    @pl.loop(0, chunks)
+    def _(chunk):
+        for n in range(len(others)):
+            block_copy(n, chunk).wait_recv()
+        part = pl.ds(pl.multiple_of(chunk * CHUNK, CHUNK), CHUNK)
+        for first, across, down, start in spans:
+            total[start : start + down, 0:across] += dot_nt(
+                local[0:down, part], local[first : first + across, part]
+            )
+
+    keep = pltpu.make_async_copy(local, gathered_ref, out_sem)
+    keep.start()
+
+    length = total.shape[0]
+    base = 0
+    slot = 0
+    at = 0
+    bases = []
+    for count, index, place in groups:
+        piece = length // count
+        copies = []
+        for k in range(1, count):
+            to = (index + k) % count
+            copies.append(pltpu.make_async_remote_copy(
+                src_ref=total.at[pl.ds(pl.multiple_of(base + to * piece, 8), piece), :],
+                dst_ref=halves.at[at + (k - 1) * piece : at + k * piece, :],
+                send_sem=rs_send.at[slot + k - 1],
+                recv_sem=rs_arrive.at[slot + k - 1],
+                device_id=place(to),
+                device_id_type=MESH,
+            ))
+            copies[-1].start()
+        for copy in copies:
+            copy.wait()
+        bases.append((base, slot, length))
+        base = base + index * piece
+        kept = pl.ds(pl.multiple_of(base, 8), piece)
+        value = total[kept, :]
+        for k in range(1, count):
+            value = value + halves[at + (k - 1) * piece : at + k * piece, :]
+        total[kept, :] = value
+        at += (count - 1) * piece
+        slot += count - 1
+        length = piece
+    final = pl.ds(pl.multiple_of(base, 8), length)
+    packed_ref[final, :] = total[final, :]
+    sent = []
+    for (count, index, place), (outer, slot, length) in zip(reversed(groups), reversed(bases)):
+        piece = length // count
+        block = pl.ds(pl.multiple_of(outer + index * piece, 8), piece)
+        copies = []
+        for k in range(1, count):
+            copies.append(pltpu.make_async_remote_copy(
+                src_ref=packed_ref.at[block, :],
+                dst_ref=packed_ref.at[block, :],
+                send_sem=ag_send.at[slot + k - 1],
+                recv_sem=ag_arrive.at[slot + k - 1],
+                device_id=place((index + k) % count),
+                device_id_type=MESH,
+            ))
+            copies[-1].start()
+        for k in range(1, count):
+            theirs = pl.ds(pl.multiple_of(outer + ((index - k + count) % count) * piece, 8), piece)
+            pltpu.make_async_remote_copy(
+                src_ref=packed_ref.at[block, :],
+                dst_ref=packed_ref.at[theirs, :],
+                send_sem=ag_send.at[slot + k - 1],
+                recv_sem=ag_arrive.at[slot + k - 1],
+                device_id=place((index + k) % count),
+                device_id_type=MESH,
+            ).wait_recv()
+        sent += copies
+    for copy in sent:
+        copy.wait_send()
+
+    @pl.loop(0, chunks)
+    def _(chunk):
+        for n in range(len(others)):
+            block_copy(n, chunk).wait_send()
+
+    keep.wait()
+
+
+def gather_and_gram(slab, row_size, col_size):
+    rows, columns = slab.shape
+    size, width = rows * row_size, columns // row_size
+    devices = row_size * col_size
+    packed = strips(size)[1]
+    packed = -(-packed // (8 * devices)) * 8 * devices
+    x_size, y_size, z_size = row_size // 2, 2, col_size // 2
+    steps = (2 - 1) + (x_size - 1) + (y_size - 1) + (z_size - 1)
+    dma = pltpu.SemaphoreType.DMA
+    return pl.pallas_call(
+        functools.partial(gram_kernel, x_size, y_size, z_size),
+        out_shape=(
+            jax.ShapeDtypeStruct((size, width), jnp.float32),
+            jax.ShapeDtypeStruct((packed, LANES), jnp.float32),
+        ),
+        in_specs=[pl.BlockSpec(memory_space=pl.ANY)],
+        out_specs=(pl.BlockSpec(memory_space=pl.ANY), pl.BlockSpec(memory_space=pltpu.VMEM)),
+        scratch_shapes=[
+            pltpu.VMEM((size, width), jnp.float32),
+            pltpu.VMEM((packed, LANES), jnp.float32),
+            pltpu.VMEM((packed, LANES), jnp.float32),
+            dma((row_size - 1, width // CHUNK)),
+            dma((row_size - 1, width // CHUNK)),
+            dma(()),
+            dma(()),
+            dma((steps,)),
+            dma((steps,)),
+            dma((steps,)),
+            dma((steps,)),
+        ],
+        compiler_params=pltpu.CompilerParams(
+            vmem_limit_bytes=40 * 1024 * 1024, collective_id=0, has_side_effects=True
+        ),
+        name="gather_and_gram",
+    )(slab)
+
+
+def unpack(packed_ref, gram):
+    spans, _ = strips(gram.shape[0])
+    for first, across, down, start in spans:
+        gram[0:down, first : first + across] = packed_ref[start : start + down, 0:across]
+        if first:
+            gram[first : first + across, 0:first] = packed_ref[start : start + first, 0:across].T
+
+
+def iterate_kernel(packed_ref, gathered_ref, start_ref, core_ref, out_ref, mapped, gram_ref, gathered, sem):
+    fetch = pltpu.make_async_copy(gathered_ref, gathered, sem)
+    fetch.start()
+    unpack(packed_ref, gram_ref)
+    mapped[...] = dot(start_ref[...], gram_ref[...])
 
     @pl.loop(0, ITERS - 1)
     def _(step):
@@ -74,33 +281,60 @@
 
     current = mapped[...]
     inverse = inverse_factor(dot_nt(current, current))
-    out_ref[...] = dot(inverse, current)
-
-
-def iterate(gram, start):
-    size, rank = start.shape
+    leading = dot(inverse, current)
+    out_ref[...] = leading
+    fetch.wait()
+    core_ref[...] = dot(leading, gathered[...])
+
+
+def iterate(packed, gathered, start):
+    rank, size = start.shape
+    width = gathered.shape[1]
+    vmem = pl.BlockSpec(memory_space=pltpu.VMEM)
     return pl.pallas_call(
         iterate_kernel,
-        out_shape=jax.ShapeDtypeStruct((rank, size), jnp.float32),
-        in_specs=[pl.BlockSpec(memory_space=pltpu.VMEM)] * 2,
-        out_specs=pl.BlockSpec(memory_space=pltpu.VMEM),
-        scratch_shapes=[pltpu.VMEM((rank, size), jnp.float32)],
-        compiler_params=pltpu.CompilerParams(vmem_limit_bytes=32 * 1024 * 1024),
+        out_shape=(
+            jax.ShapeDtypeStruct((rank, width), jnp.float32),
+            jax.ShapeDtypeStruct((rank, size), jnp.float32),
+        ),
+        in_specs=[vmem, pl.BlockSpec(memory_space=pl.ANY), vmem],
+        out_specs=(vmem, vmem),
+        scratch_shapes=[
+            pltpu.VMEM((rank, size), jnp.float32),
+            pltpu.VMEM((size, size), jnp.float32),
+            pltpu.VMEM((size, width), jnp.float32),
+            pltpu.SemaphoreType.DMA(()),
+        ],
+        compiler_params=pltpu.CompilerParams(vmem_limit_bytes=40 * 1024 * 1024),
         name="iterate",
-    )(gram, start)
-
-
-def shards(field_slab, start_basis):
-    gathered = lax.all_to_all(field_slab, "row", split_axis=2, concat_axis=0, tiled=True)
-    flat = gathered.reshape(gathered.shape[0], -1)
-    local_gram = dot_nt(flat, flat)
-    gram_total = lax.psum(local_gram, ("row", "col"))
-    leading_t = iterate(gram_total, start_basis)
-    core = dot(leading_t, flat)
-    return (core.reshape((-1,) + gathered.shape[1:]), leading_t.T)
+    )(packed, gathered, start)
+
+
+def pack(gram):
+    spans, used = strips(gram.shape[0])
+    parts = [
+        jnp.pad(gram[0:down, first : first + across], ((0, 0), (0, LANES - across)))
+        for first, across, down, start in spans
+    ]
+    return jnp.concatenate(parts, axis=0)
 
 
 def solution(mesh):
+    row_size, col_size = mesh.shape["row"], mesh.shape["col"]
+
+    def shards(field_slab, start_basis):
+        rows, depth, columns = field_slab.shape
+        slab = field_slab.reshape(rows, depth * columns)
+        aligned = depth == 1 and rows % 8 == 0 and row_size % 2 == 0 and col_size % 2 == 0
+        if aligned and columns % (row_size * CHUNK) == 0:
+            gathered, packed = gather_and_gram(slab, row_size, col_size)
+        else:
+            gathered = lax.all_to_all(field_slab, "row", split_axis=2, concat_axis=0, tiled=True)
+            gathered = gathered.reshape(gathered.shape[0], -1)
+            packed = lax.psum(pack(dot_nt(gathered, gathered)), ("row", "col"))
+        core, leading_t = iterate(packed, gathered, start_basis.T)
+        return (core.reshape(core.shape[0], depth, -1), leading_t.T)
+
     placed = (P("row", "col", None), P())
     return jax.shard_map(
         shards, mesh=mesh, in_specs=placed, out_specs=(P(None, "col", "row"), P()), check_vma=False

time: 273 us -> 113 us (0.41)
  waiting for transfers between devices: 135 us -> 0 us
  Pallas kernels: 25.2 us -> 107 us
  blocking collectives: 54.5 us -> 0 us
  local copies, waits for them, and re-layouts: 32.6 us -> 5.07 us
  between operations: 14.1 us -> 0.66 us
  matrix products: 10.7 us -> 0 us
    psum x1 -> x0, waiting for transfers between devices: 135 us -> none  [shards(): gram_total = lax.psum(local_gram, ('row', 'col'))]
    pallas_call x1 -> x2, Pallas kernels: 25.2 us -> 107 us  [the longest x1 80.5 us: gather_and_gram(): pl.pallas_call(functools.partial(gram_kernel, x_size, y_size, z_size), ou...]
    all_to_all x1 -> x0, blocking collectives: 54.5 us -> none  [shards(): lax.all_to_all(field_slab, 'row', split_axis=2, concat_axis=0, tiled=True)]
    all_to_all x3 -> x0, local copies, waits for them, and re-layouts: 16 us -> none  [shards(): lax.all_to_all(field_slab, 'row', split_axis=2, concat_axis=0, tiled=True)]
    unnamed x7 -> x4, local copies, waits for them, and re-layouts: 16.6 us -> 5.07 us
    dot_general x2 -> x0, matrix products: 10.7 us -> none  [the longest x1 8.01 us: dot_nt(): lax.dot_general(a, b, (((1,), (1,)), ((), ())), precision=HIGHEST, prefer...]
  transfers between devices with their start and end apart: 1 -> 0, of which waited for: 1 -> 0; matrix products, arithmetic and copies ran while one was open for 0% -> 0% of each run, Pallas kernels for 0% -> 0%
where the time goes in v1:
time: 113 us
  Pallas kernels  107 us (95%)
  local copies, waits for them, and re-layouts  5.07 us (4%)
    pallas_call x1, Pallas kernels, gather_and_gram(): pl.pallas_call(functools.partial(gram_kernel, x_size, y_size, z_size), ou...  80.5 us
    pallas_call x1, Pallas kernels, iterate(): pl.pallas_call(iterate_kernel, out_shape=(jax.ShapeDtypeStruct((rank, wid...  26.3 us
    unnamed x4, local copies, waits for them, and re-layouts  5.07 us

profile of v1, /device:TPU:0, one launch (start us, length us, event | category | flops | bytes accessed | tf_op | source)
XLA Modules:
  0.0 112.5 jit_solution(1463173004045470699)
XLA Ops:
  0.6 4.1 %copy.7 = f32[168,1,4096]{2,0,1:T(8,128)S(1)} copy(f32[168,1,4096]{2,1,0:T(1,128)} %param.2) | data formatting | bytes 5505024
  4.7 0.0 copy-start
  4.7 80.5 %gather_and_gram.1 = (f32[672,1024]{1,0:T(8,128)S(1)}, f32[2816,128]{1,0:T(8,128)S(1)}) custom-call(f32[168,4096]{1,0:T(8,128)S(1)} %bitcast.6), custom_call_target="tpu_custom_call" | custom-call | tf_op jit(solution)/shard_map/gather_and_gram/pallas_call | solution.py:234
  85.2 0.0 copy-done
  85.2 26.3 %iterate.1 = (f32[64,1024]{1,0:T(8,128)S(1)}, f32[64,672]{1,0:T(8,128)}) custom-call(f32[2816,128]{1,0:T(8,128)S(1)} %get-tuple-element.6.packed_ref, f32[672,1024]{1,0:T(8,128)S(1)} %get-tuple-element.7.gathered_ref, f32[64,672]{1,0:T(8,128)S(1)} %bitcast.8), custom_call_target="tpu_custom_call" | custom-call | tf_op jit(solution)/shard_map/iterate/pallas_call | solution.py:294
  111.5 1.0 copy.4
Async XLA Ops:
  4.7 80.5 %copy-start = (f32[672,64]{0,1:T(8,128)S(1)}, f32[672,64]{0,1:T(8,128)}, u32[]{:S(2)}) copy-start(f32[672,64]{0,1:T(8,128)} %param.3) | copy-start | bytes 516100

commit v2 on v0

--- a/solution.py
+++ b/solution.py
@@ -62,9 +62,289 @@
     return jnp.concatenate(done, axis=0)
 
 
-def iterate_kernel(gram_ref, start_ref, out_ref, mapped):
-    gram = gram_ref[...]
-    mapped[...] = dot(start_ref[...].T, gram)
+LANES = 128
+CHUNK = 256
+MESH = pl.DeviceIdType.MESH
+
+
+def strips(size):
+    found, start = [], 0
+    for first in range(0, size, LANES):
+        width = min(LANES, size - first)
+        found.append((first, width, first + width, start))
+        start += first + width
+    return found, start
+
+
+def sizes(half, z_size):
+    own = strips(half)[1]
+    cross = half * (-(-half // LANES))
+    own_unit, cross_unit = 32 * z_size, 64 * z_size
+    return -(-own // own_unit) * own_unit, -(-cross // cross_unit) * cross_unit
+
+
+def remote(source, target, send, arrive, place):
+    return pltpu.make_async_remote_copy(
+        src_ref=source, dst_ref=target, send_sem=send, recv_sem=arrive,
+        device_id=place, device_id_type=MESH,
+    )
+
+
+def reduce_scatter(total, landing, groups, send, arrive):
+    length, base, slot, at, levels = total.shape[0], 0, 0, 0, []
+    for count, index, place in groups:
+        piece = length // count
+        copies = []
+        for k in range(1, count):
+            to = (index + k) % count
+            copies.append(remote(
+                total.at[pl.ds(pl.multiple_of(base + to * piece, 8), piece), :],
+                landing.at[at + (k - 1) * piece : at + k * piece, :],
+                send.at[slot + k - 1], arrive.at[slot + k - 1], place(to),
+            ))
+            copies[-1].start()
+        for copy in copies:
+            copy.wait()
+        levels.append((base, slot, length))
+        base = base + index * piece
+        kept = pl.ds(pl.multiple_of(base, 8), piece)
+        value = total[kept, :]
+        for k in range(1, count):
+            value = value + landing[at + (k - 1) * piece : at + k * piece, :]
+        total[kept, :] = value
+        at += (count - 1) * piece
+        slot += count - 1
+        length = piece
+    return base, length, levels
+
+
+def all_gather(result, offset, groups, levels, send, arrive):
+    sent = []
+    for (count, index, place), (outer, slot, length) in zip(reversed(groups), reversed(levels)):
+        piece = length // count
+
+        def block(i):
+            rows = pl.ds(pl.multiple_of(offset + outer + i * piece, 8), piece)
+            return result.at[rows, :]
+
+        for k in range(1, count):
+            sent.append(remote(
+                block(index), block(index), send.at[slot + k - 1], arrive.at[slot + k - 1],
+                place((index + k) % count),
+            ))
+            sent[-1].start()
+        for k in range(1, count):
+            theirs = block((index - k + count) % count)
+            remote(
+                theirs, theirs, send.at[slot + k - 1], arrive.at[slot + k - 1],
+                place((index + k) % count),
+            ).wait_recv()
+    return sent
+
+
+def gram_kernel(
+    y_size, z_size, slab_ref, gathered_ref, packed_ref,
+    local, extra, own_total, own_landing, cross_total, cross_landing,
+    sib_send, sib_arrive, send, arrive, own_sem, out_sem,
+    own_rs, own_rs_in, own_ag, own_ag_in, cross_rs, cross_rs_in, cross_ag, cross_ag_in,
+    swap, swap_in,
+):
+    rows, columns = slab_ref.shape
+    width, half = columns // 4, 2 * rows
+    row, col = lax.axis_index("row"), lax.axis_index("col")
+    x, core = row // 2, row % 2
+    z, y = col // y_size, col % y_size
+    sibling = {"row": x * 2 + 1 - core}
+    across_x = {"row": (1 - x) * 2 + core}
+    by_core = (2, core, lambda i: {"row": x * 2 + i})
+    by_x = (2, x, lambda i: {"row": i * 2 + core})
+    by_y = (y_size, y, lambda i: {"col": z * y_size + i})
+    by_z = (z_size, z, lambda i: {"col": i * y_size + y})
+
+    barrier = pltpu.get_barrier_semaphore()
+    partners = [sibling] + [{"row": (1 - x) * 2 + i} for i in range(2)]
+    for count, index, place in (by_y, by_z):
+        partners += [place((index + k) % count) for k in range(1, count)]
+    for partner in partners:
+        pl.semaphore_signal(barrier, inc=1, device_id=partner, device_id_type=MESH)
+    pl.semaphore_wait(barrier, len(partners))
+
+    def columns_of(r):
+        return slab_ref.at[:, pl.ds(pl.multiple_of(r * width, width), width)]
+
+    my_rows = pl.ds(pl.multiple_of(row * rows, 8), rows)
+    my_half_rows = pl.ds(pl.multiple_of(core * rows, 8), rows)
+    siblings = [
+        remote(columns_of(x * 2 + 1 - core), local.at[my_rows, :],
+               sib_send.at[0], sib_arrive.at[0], sibling),
+        remote(columns_of((1 - x) * 2 + 1 - core), extra.at[my_half_rows, :],
+               sib_send.at[1], sib_arrive.at[1], sibling),
+    ]
+    chunks = width // CHUNK
+
+    def block_copy(n, chunk):
+        to = (1 - x) * 2 + (core + n) % 2
+        return remote(
+            slab_ref.at[:, pl.ds(pl.multiple_of(to * width + chunk * CHUNK, CHUNK), CHUNK)],
+            local.at[my_rows, pl.ds(pl.multiple_of(chunk * CHUNK, CHUNK), CHUNK)],
+            send.at[n, chunk], arrive.at[n, chunk], {"row": to},
+        )
+
+    for copy in siblings:
+        copy.start()
+    for chunk in range(chunks):
+        for n in range(2):
+            block_copy(n, chunk).start()
+    mine = [
+        pltpu.make_async_copy(columns_of(row), local.at[my_rows, :], own_sem.at[0]),
+        pltpu.make_async_copy(
+            columns_of((1 - x) * 2 + core), extra.at[my_half_rows, :], own_sem.at[1]
+        ),
+    ]
+    for copy in mine:
+        copy.start()
+    own_total[...] = jnp.zeros_like(own_total)
+    cross_total[...] = jnp.zeros_like(cross_total)
+    for copy in mine:
+        copy.wait()
+    for copy in siblings:
+        copy.wait()
+    spans, _ = strips(half)
+
+    @pl.loop(0, chunks)
+    def _(chunk):
+        part = pl.ds(pl.multiple_of(chunk * CHUNK, CHUNK), CHUNK)
+        for first, across, down, start in spans:
+            upper = pl.ds(pl.multiple_of(x * half, 8), down)
+            lower = pl.ds(pl.multiple_of(x * half + first, 8), across)
+            own_total[start : start + down, 0:across] += dot_nt(
+                local[upper, part], local[lower, part]
+            ) + dot_nt(extra[0:down, part], extra[first : first + across, part])
+
+    own_groups = [by_core, by_y, by_z]
+    own_size = own_total.shape[0]
+    share = own_size // 2
+    offset = x * own_size
+    base, length, levels = reduce_scatter(own_total, own_landing, own_groups, own_rs, own_rs_in)
+    packed_ref[pl.ds(pl.multiple_of(offset + base, 8), length), :] = own_total[
+        pl.ds(pl.multiple_of(base, 8), length), :
+    ]
+    sent = all_gather(packed_ref, offset, own_groups[1:], levels[1:], own_ag, own_ag_in)
+
+    def share_of(i, half_index):
+        begin = pl.multiple_of(i * own_size + half_index * share, 8)
+        return packed_ref.at[pl.ds(begin, share), :]
+
+    swaps = [
+        remote(share_of(x, core), share_of(x, core), swap.at[0], swap_in.at[0], sibling),
+        remote(share_of(x, core), share_of(x, core), swap.at[1], swap_in.at[1], across_x),
+    ]
+    for copy in swaps:
+        copy.start()
+
+    @pl.loop(0, chunks)
+    def _(chunk):
+        for n in range(2):
+            block_copy(n, chunk).wait_recv()
+        part = pl.ds(pl.multiple_of(chunk * CHUNK, CHUNK), CHUNK)
+        for j, (first, across, _, _) in enumerate(spans):
+            cross_total[j * half : (j + 1) * half, 0:across] += dot_nt(
+                local[0:half, part], local[half + first : half + first + across, part]
+            )
+
+    keep = pltpu.make_async_copy(local, gathered_ref, out_sem)
+    keep.start()
+    cross_groups = [by_core, by_y, by_z, by_x]
+    base, length, levels = reduce_scatter(
+        cross_total, cross_landing, cross_groups, cross_rs, cross_rs_in
+    )
+    packed_ref[pl.ds(pl.multiple_of(2 * own_size + base, 8), length), :] = cross_total[
+        pl.ds(pl.multiple_of(base, 8), length), :
+    ]
+    remote(share_of(1 - x, core), share_of(1 - x, core), swap.at[1], swap_in.at[1],
+           across_x).wait_recv()
+    swaps.append(remote(share_of(1 - x, core), share_of(1 - x, core), swap.at[2], swap_in.at[2],
+                        sibling))
+    swaps[-1].start()
+    sent += all_gather(packed_ref, 2 * own_size, cross_groups, levels, cross_ag, cross_ag_in)
+    remote(share_of(x, 1 - core), share_of(x, 1 - core), swap.at[0], swap_in.at[0],
+           sibling).wait_recv()
+    remote(share_of(1 - x, 1 - core), share_of(1 - x, 1 - core), swap.at[2], swap_in.at[2],
+           sibling).wait_recv()
+    for copy in sent + swaps:
+        copy.wait_send()
+
+    @pl.loop(0, chunks)
+    def _(chunk):
+        for n in range(2):
+            block_copy(n, chunk).wait_send()
+
+    keep.wait()
+
+
+def gather_and_gram(slab, col_size):
+    rows, columns = slab.shape
+    half, width = 2 * rows, columns // 4
+    y_size, z_size = 2, col_size // 2
+    own_size, cross_size = sizes(half, z_size)
+    own_steps, cross_steps = 1 + 1 + (z_size - 1), 1 + 1 + (z_size - 1) + 1
+    dma = pltpu.SemaphoreType.DMA
+    f32 = lambda *shape: pltpu.VMEM(shape, jnp.float32)
+    return pl.pallas_call(
+        functools.partial(gram_kernel, y_size, z_size),
+        out_shape=(
+            jax.ShapeDtypeStruct((2 * half, width), jnp.float32),
+            jax.ShapeDtypeStruct((2 * own_size + cross_size, LANES), jnp.float32),
+        ),
+        in_specs=[pl.BlockSpec(memory_space=pl.ANY)],
+        out_specs=(pl.BlockSpec(memory_space=pl.ANY), pl.BlockSpec(memory_space=pltpu.VMEM)),
+        scratch_shapes=[
+            f32(2 * half, width), f32(half, width),
+            f32(own_size, LANES), f32(own_size, LANES),
+            f32(cross_size, LANES), f32(cross_size, LANES),
+            dma((2,)), dma((2,)),
+            dma((2, width // CHUNK)), dma((2, width // CHUNK)),
+            dma((2,)), dma(()),
+        ] + [dma((own_steps,))] * 4 + [dma((cross_steps,))] * 4 + [dma((3,))] * 2,
+        compiler_params=pltpu.CompilerParams(
+            vmem_limit_bytes=40 * 1024 * 1024, collective_id=0, has_side_effects=True
+        ),
+        name="gather_and_gram",
+    )(slab)
+
+
+def unpack(packed_ref, gram, half, own_size):
+    spans, _ = strips(half)
+    padded = gram.shape[0] // 2
+    gram[...] = jnp.zeros_like(gram)
+    for i in range(2):
+        for first, across, down, start in spans:
+            at, edge = i * own_size + start, i * padded
+            column = edge + first
+            gram[edge : edge + down, column : column + LANES] = packed_ref[at : at + down, :]
+            if first:
+                gram[column : column + LANES, edge : edge + first] = packed_ref[
+                    at : at + first, :
+                ].T
+    for j, (first, _, _, _) in enumerate(spans):
+        at, column = 2 * own_size + j * half, padded + first
+        block = packed_ref[at : at + half, :]
+        gram[0:half, column : column + LANES] = block
+        gram[column : column + LANES, 0:half] = block.T
+
+
+def iterate_kernel(
+    own_size, packed_ref, gathered_ref, start_ref, core_ref, out_ref, mapped, gram_ref, gathered, sem
+):
+    fetch = pltpu.make_async_copy(gathered_ref, gathered, sem)
+    fetch.start()
+    rank, size = start_ref.shape
+    half, padded = size // 2, gram_ref.shape[0] // 2
+    unpack(packed_ref, gram_ref, half, own_size)
+    gap = jnp.zeros((rank, padded - half), jnp.float32)
+    start = start_ref[...]
+    start = jnp.concatenate([start[:, :half], gap, start[:, half:], gap], axis=1)
+    mapped[...] = dot(start, gram_ref[...])
 
     @pl.loop(0, ITERS - 1)
     def _(step):
@@ -74,33 +354,70 @@
 
     current = mapped[...]
     inverse = inverse_factor(dot_nt(current, current))
-    out_ref[...] = dot(inverse, current)
-
-
-def iterate(gram, start):
-    size, rank = start.shape
+    leading = dot(inverse, current)
+    leading = jnp.concatenate([leading[:, :half], leading[:, padded : padded + half]], axis=1)
+    out_ref[...] = leading
+    fetch.wait()
+    core_ref[...] = dot(leading, gathered[...])
+
+
+def iterate(packed, gathered, start, own_size):
+    rank, size = start.shape
+    width = gathered.shape[1]
+    padded = 2 * LANES * (-(-size // (2 * LANES)))
+    vmem = pl.BlockSpec(memory_space=pltpu.VMEM)
     return pl.pallas_call(
-        iterate_kernel,
-        out_shape=jax.ShapeDtypeStruct((rank, size), jnp.float32),
-        in_specs=[pl.BlockSpec(memory_space=pltpu.VMEM)] * 2,
-        out_specs=pl.BlockSpec(memory_space=pltpu.VMEM),
-        scratch_shapes=[pltpu.VMEM((rank, size), jnp.float32)],
-        compiler_params=pltpu.CompilerParams(vmem_limit_bytes=32 * 1024 * 1024),
+        functools.partial(iterate_kernel, own_size),
+        out_shape=(
+            jax.ShapeDtypeStruct((rank, width), jnp.float32),
+            jax.ShapeDtypeStruct((rank, size), jnp.float32),
+        ),
+        in_specs=[vmem, pl.BlockSpec(memory_space=pl.ANY), vmem],
+        out_specs=(vmem, vmem),
+        scratch_shapes=[
+            pltpu.VMEM((rank, padded), jnp.float32),
+            pltpu.VMEM((padded, padded), jnp.float32),
+            pltpu.VMEM((size, width), jnp.float32),
+            pltpu.SemaphoreType.DMA(()),
+        ],
+        compiler_params=pltpu.CompilerParams(vmem_limit_bytes=40 * 1024 * 1024),
         name="iterate",
-    )(gram, start)
-
-
-def shards(field_slab, start_basis):
-    gathered = lax.all_to_all(field_slab, "row", split_axis=2, concat_axis=0, tiled=True)
-    flat = gathered.reshape(gathered.shape[0], -1)
-    local_gram = dot_nt(flat, flat)
-    gram_total = lax.psum(local_gram, ("row", "col"))
-    leading_t = iterate(gram_total, start_basis)
-    core = dot(leading_t, flat)
-    return (core.reshape((-1,) + gathered.shape[1:]), leading_t.T)
+    )(packed, gathered, start)
+
+
+def pack(gram, own_size, cross_size):
+    half = gram.shape[0] // 2
+    spans, used = strips(half)
+    wide = lambda part, across: jnp.pad(part, ((0, 0), (0, LANES - across)))
+    parts = []
+    for i in range(2):
+        own = gram[i * half : (i + 1) * half, i * half : (i + 1) * half]
+        parts += [wide(own[0:down, a : a + w], w) for a, w, down, _ in spans]
+        parts.append(jnp.zeros((own_size - used, LANES), jnp.float32))
+    cross = gram[:half, half:]
+    parts += [wide(cross[:, a : a + w], w) for a, w, _, _ in spans]
+    parts.append(jnp.zeros((cross_size - half * len(spans), LANES), jnp.float32))
+    return jnp.concatenate(parts, axis=0)
 
 
 def solution(mesh):
+    row_size, col_size = mesh.shape["row"], mesh.shape["col"]
+
+    def shards(field_slab, start_basis):
+        rows, depth, columns = field_slab.shape
+        slab = field_slab.reshape(rows, depth * columns)
+        own_size, cross_size = sizes(rows * row_size // 2, col_size // 2)
+        aligned = depth == 1 and rows % 8 == 0 and row_size == 4 and col_size % 2 == 0
+        if aligned and columns % (row_size * CHUNK) == 0:
+            gathered, packed = gather_and_gram(slab, col_size)
+        else:
+            gathered = lax.all_to_all(field_slab, "row", split_axis=2, concat_axis=0, tiled=True)
+            gathered = gathered.reshape(gathered.shape[0], -1)
+            packed = pack(dot_nt(gathered, gathered), own_size, cross_size)
+            packed = lax.psum(packed, ("row", "col"))
+        core, leading_t = iterate(packed, gathered, start_basis.T, own_size)
+        return (core.reshape(core.shape[0], depth, -1), leading_t.T)
+
     placed = (P("row", "col", None), P())
     return jax.shard_map(
         shards, mesh=mesh, in_specs=placed, out_specs=(P(None, "col", "row"), P()), check_vma=False

time: 273 us -> 96.2 us (0.35)
  waiting for transfers between devices: 135 us -> 0 us
  Pallas kernels: 25.2 us -> 90.4 us
  blocking collectives: 54.5 us -> 0 us
  local copies, waits for them, and re-layouts: 32.6 us -> 5.07 us
  between operations: 14.1 us -> 0.66 us
  matrix products: 10.7 us -> 0 us
    psum x1 -> x0, waiting for transfers between devices: 135 us -> none  [shards(): gram_total = lax.psum(local_gram, ('row', 'col'))]
    pallas_call x1 -> x2, Pallas kernels: 25.2 us -> 90.4 us  [the longest x1 64.5 us: gather_and_gram(): pl.pallas_call(functools.partial(gram_kernel, y_size, z_size), out_shape=...]
    all_to_all x1 -> x0, blocking collectives: 54.5 us -> none  [shards(): lax.all_to_all(field_slab, 'row', split_axis=2, concat_axis=0, tiled=True)]
    all_to_all x3 -> x0, local copies, waits for them, and re-layouts: 16 us -> none  [shards(): lax.all_to_all(field_slab, 'row', split_axis=2, concat_axis=0, tiled=True)]
    unnamed x7 -> x4, local copies, waits for them, and re-layouts: 16.6 us -> 5.07 us
    dot_general x2 -> x0, matrix products: 10.7 us -> none  [the longest x1 8.01 us: dot_nt(): lax.dot_general(a, b, (((1,), (1,)), ((), ())), precision=HIGHEST, prefer...]
  transfers between devices with their start and end apart: 1 -> 0, of which waited for: 1 -> 0; matrix products, arithmetic and copies ran while one was open for 0% -> 0% of each run, Pallas kernels for 0% -> 0%
where the time goes in v2:
time: 96.2 us; the launch traced here: 96.1 us
  Pallas kernels  90.4 us (94%)
  local copies, waits for them, and re-layouts  5.07 us (5%)
    pallas_call x1, Pallas kernels, gather_and_gram(): pl.pallas_call(functools.partial(gram_kernel, y_size, z_size), out_shape=...  64.5 us
    pallas_call x1, Pallas kernels, iterate(): pl.pallas_call(functools.partial(iterate_kernel, own_size), out_shape=(ja...  25.9 us
    unnamed x4, local copies, waits for them, and re-layouts  5.07 us

profile of v2, /device:TPU:0, one launch (start us, length us, event | category | flops | bytes accessed | tf_op | source)
XLA Modules:
  0.0 96.1 jit_solution(17549739364026809982)
XLA Ops:
  0.6 4.1 %copy.7 = f32[168,1,4096]{2,0,1:T(8,128)S(1)} copy(f32[168,1,4096]{2,1,0:T(1,128)} %param.2) | data formatting | bytes 5505024
  4.7 0.0 copy-start
  4.7 64.5 %gather_and_gram.1 = (f32[672,1024]{1,0:T(8,128)S(1)}, f32[2560,128]{1,0:T(8,128)S(1)}) custom-call(f32[168,4096]{1,0:T(8,128)S(1)} %bitcast.6), custom_call_target="tpu_custom_call" | custom-call | tf_op jit(solution)/shard_map/gather_and_gram/pallas_call | solution.py:293
  69.2 0.0 copy-done
  69.2 25.9 %iterate.1 = (f32[64,1024]{1,0:T(8,128)S(1)}, f32[64,672]{1,0:T(8,128)}) custom-call(f32[2560,128]{1,0:T(8,128)S(1)} %get-tuple-element.6.packed_ref, f32[672,1024]{1,0:T(8,128)S(1)} %get-tuple-element.7.gathered_ref, f32[64,672]{1,0:T(8,128)S(1)} %bitcast.8), custom_call_target="tpu_custom_call" | custom-call | tf_op jit(solution)/shard_map/iterate/pallas_call | solution.py:369
  95.1 1.0 %copy.4 = f32[64,1,1024]{2,1,0:T(1,128)} copy(f32[64,1,1024]{2,0,1:T(8,128)S(1)} %bitcast.7) | data formatting | bytes 524288
Async XLA Ops:
  4.7 64.5 %copy-start = (f32[672,64]{0,1:T(8,128)S(1)}, f32[672,64]{0,1:T(8,128)}, u32[]{:S(2)}) copy-start(f32[672,64]{0,1:T(8,128)} %param.3) | copy-start | bytes 516100
